TPU v7x, 1024 devices: a whole 8x8x8 slice. The times are simulated.
1024 devices in a mesh: dp: 128 (over x, y, core), blk: 8 (over z).
Axes of the slice: x: 8, y: 8, z: 8, core: 2. Of those that a mesh axis runs over, the one named last changes fastest.
Arguments:
- inputs: bfloat16 [1280, 8192], P(None, 'dp'), may hold values from -3 to 3
- grad_out: bfloat16 [1280, 8192], P(None, 'dp'), may hold values from -3 to 3
- up_weight: bfloat16 [8192, 28672], P('dp', 'blk'), may hold values from -0.0625 to 0.0625
- gate_weight: bfloat16 [8192, 28672], P('dp', 'blk'), may hold values from -0.0625 to 0.0625
- down_weight: bfloat16 [28672, 8192], P('blk', 'dp'), may hold values from -0.0625 to 0.0625
- saved_gate: bfloat16 [8, 30, 128, 128], P('blk'), may hold values from -6 to 6
- saved_up: bfloat16 [8, 30, 128, 128], P('blk'), may hold values from -6 to 6
- block_ids: int32 [10, 24], replicated, may hold values from 0 to 223, as said below
- counts: int32 [10], replicated, may hold values from 3 to 24, as said below
Outputs:
- grad_x: bfloat16 [1280, 8192], P('blk', 'dp')
- grad_w_up: bfloat16 [8192, 28672], P('dp', 'blk')
- grad_w_gate: bfloat16 [8192, 28672], P('dp', 'blk')
- grad_w_down: bfloat16 [28672, 8192], P('blk', 'dp')
Inputs may be any that keep to these rules, and one draw needn't show every extreme that they name: `block_ids`: entries k < counts[t] of tile t's list are live and name distinct blocks; later entries are unused. The live entries of one tile name at most 3 blocks of any one owner (block b belongs to owner b // 28); over all tiles the live entries naming one owner's blocks number at most 30, and in every draw some owner reaches 30. `counts`: in every draw some tile has 24 live entries.
All inputs are finite; a program needn't handle non-finite values.
Results may differ from a plain program's by a relative error of at most 0.0057.
Values may be sent and summed in bfloat16 or wider, within the bound.
A program may use at most 32 MiB of HBM per device.

v0:
```python
import jax
import jax.numpy as jnp
from jax import lax
from jax.sharding import PartitionSpec as P


def compact(block_ids, counts, owner_index, own_blocks, capacity):
    tile_count = block_ids.shape[0]
    list_len = block_ids.shape[1]
    entries = jnp.arange(list_len, dtype=jnp.int32)
    live_entry = entries[None, :] < counts[:, None]
    owned_entry = (
        (live_entry & (block_ids // own_blocks == owner_index)).reshape(-1).astype(jnp.int32)
    )
    position = jnp.cumsum(owned_entry) - 1
    slot_index = jnp.arange(capacity, dtype=jnp.int32)
    matches = (owned_entry[None, :] == 1) & (position[None, :] == slot_index[:, None])
    pair_index = jnp.arange(tile_count * list_len, dtype=jnp.int32)
    chosen = jnp.sum(jnp.where(matches, pair_index[None, :], 0), axis=1)
    slot_live = jnp.sum(matches.astype(jnp.int32), axis=1)
    tile_of = chosen // list_len
    block_id = jnp.take(block_ids.reshape(-1), chosen)
    local_block = jnp.where(slot_live > 0, block_id - owner_index * own_blocks, 0)
    return (tile_of, local_block, slot_live)


def slot_grads(gate_in, up_in, slot_live, grad_hidden):
    gate_value = gate_in.astype(jnp.float32)
    up_value = up_in.astype(jnp.float32)
    mask_value = slot_live.astype(jnp.float32)[:, None, None]
    grad_value = grad_hidden.astype(jnp.float32)
    hidden = (jax.nn.relu(gate_value) * up_value * mask_value).astype(jnp.bfloat16)
    grad_gate = (grad_value * up_value * (gate_value > 0).astype(jnp.float32) * mask_value).astype(
        jnp.bfloat16
    )
    grad_up = (grad_value * jax.nn.relu(gate_value) * mask_value).astype(jnp.bfloat16)
    return (hidden, grad_gate, grad_up)


def shards(
    inputs, grad_out, up_weight, gate_weight, down_weight, saved_gate, saved_up, block_ids, counts
):
    model_width = inputs.shape[1]
    capacity = saved_gate.shape[1]
    tile_len = saved_gate.shape[2]
    block_len = saved_gate.shape[3]
    tile_count = block_ids.shape[0]
    own_blocks = down_weight.shape[0] // block_len
    highest = lax.Precision.HIGHEST
    owner_index = lax.axis_index("blk")
    tile_of, local_block, slot_live = compact(block_ids, counts, owner_index, own_blocks, capacity)
    input_slots = jnp.take(inputs.reshape(tile_count, tile_len, model_width), tile_of, axis=0)
    grad_slots = jnp.take(grad_out.reshape(tile_count, tile_len, model_width), tile_of, axis=0)
    down_slots = jnp.take(
        down_weight.reshape(own_blocks, block_len, model_width), local_block, axis=0
    )
    up_slots = jnp.take(up_weight.reshape(model_width, own_blocks, block_len), local_block, axis=1)
    gate_slots = jnp.take(
        gate_weight.reshape(model_width, own_blocks, block_len), local_block, axis=1
    )
    hidden_terms = jnp.einsum(
        "std,sbd->stb", grad_slots, down_slots, preferred_element_type=jnp.float32
    )
    hidden_terms = hidden_terms.reshape(capacity * tile_len, block_len)
    grad_hidden = lax.psum(hidden_terms, "dp").astype(jnp.bfloat16)
    grad_hidden = grad_hidden.reshape(capacity, tile_len, block_len)
    hidden, grad_gate, grad_up = slot_grads(saved_gate[0], saved_up[0], slot_live, grad_hidden)
    owned_block = (
        (local_block[:, None] == jnp.arange(own_blocks, dtype=jnp.int32)[None, :])
        & (slot_live[:, None] > 0)
    ).astype(jnp.float32)
    down_terms = jnp.einsum("stb,std->sbd", hidden, grad_slots, preferred_element_type=jnp.float32)
    down_sum = jnp.einsum("so,sbd->obd", owned_block, down_terms, precision=highest)
    grad_w_down = down_sum.reshape(own_blocks * block_len, model_width).astype(jnp.bfloat16)
    up_terms = jnp.einsum("std,stb->sdb", input_slots, grad_up, preferred_element_type=jnp.float32)
    up_sum = jnp.einsum("so,sdb->dob", owned_block, up_terms, precision=highest)
    grad_w_up = up_sum.reshape(model_width, own_blocks * block_len).astype(jnp.bfloat16)
    gate_terms = jnp.einsum(
        "std,stb->sdb", input_slots, grad_gate, preferred_element_type=jnp.float32
    )
    gate_sum = jnp.einsum("so,sdb->dob", owned_block, gate_terms, precision=highest)
    grad_w_gate = gate_sum.reshape(model_width, own_blocks * block_len).astype(jnp.bfloat16)
    input_terms = jnp.einsum(
        "stb,dsb->std", grad_gate, gate_slots, preferred_element_type=jnp.float32
    )
    input_terms = input_terms + jnp.einsum(
        "stb,dsb->std", grad_up, up_slots, preferred_element_type=jnp.float32
    )
    tile_match = (
        (tile_of[:, None] == jnp.arange(tile_count, dtype=jnp.int32)[None, :])
        & (slot_live[:, None] > 0)
    ).astype(jnp.float32)
    input_part = jnp.einsum("sn,std->ntd", tile_match, input_terms, precision=highest)
    input_part = input_part.reshape(tile_count * tile_len, model_width)
    grad_x = lax.psum_scatter(input_part, "blk", scatter_dimension=0, tiled=True).astype(
        jnp.bfloat16
    )
    return (grad_x, grad_w_up, grad_w_gate, grad_w_down)


def solution(mesh):
    in_specs = (
        P(None, "dp"),
        P(None, "dp"),
        P("dp", "blk"),
        P("dp", "blk"),
        P("blk", "dp"),
        P("blk", None, None, None),
        P("blk", None, None, None),
        P(),
        P(),
    )
    out_specs = (P("blk", "dp"), P("dp", "blk"), P("dp", "blk"), P("blk", "dp"))
    return jax.shard_map(shards, mesh=mesh, in_specs=in_specs, out_specs=out_specs, check_vma=False)
```

profile of v0, /device:TPU:1, one launch (start us, length us, event | category | flops | bytes accessed | tf_op | source)
XLA Modules:
  0.0 594.8 jit_solution(2080166856022180874)
XLA Ops:
  7.2 0.0 copy-start
  7.2 0.0 reduce-scatter.4.cloned.1.call-start
  7.2 0.8 fusion.45
  8.0 0.1 reshape.185
  8.1 0.8 reshape.178
  8.9 0.3 reduce-window.9
  9.2 0.1 slice.10
  9.3 0.1 slice_reduce_fusion
  9.5 0.1 add_bitcast_fusion
  9.5 0.1 convert_reduce_fusion
  9.7 0.7 gather_fusion
  10.5 0.9 copy_bitcast_fusion.7
  11.5 0.0 copy-done
  11.5 0.1 copy_bitcast_fusion.5
  11.6 0.6 gather_fusion.2
  12.2 0.0 copy-start.2
  12.3 0.6 gather_fusion.1
  12.9 1.8 fusion.24
  14.7 0.0 copy-done.2
  14.7 0.0 copy-start.8
  14.7 517.4 %all-reduce.2 = bf16[3840,128]{1,0:T(8,128)(2,1)S(1)} all-reduce(f32[3840,128]{1,0:T(8,128)} %bitcast.119), channel_id=1, replica_groups=mesh['dp'=128,'blk'=8] {'dp'}, use_global_device_ids=true, to_apply=%region_4.6 | all-reduce | flops 491520 | bytes 2949120 | tf_op jit(solution)/shard_map/psum | solution.py:65
  532.2 0.0 copy-done.8
  532.2 0.0 copy-start.1
  532.2 0.1 copy_bitcast_fusion.4
  532.4 1.2 copy_bitcast_fusion.3
  533.6 1.4 gather_fusion.3
  534.9 1.4 gather_fusion.4
  536.3 0.0 copy-done.1
  536.3 0.0 copy-start.7
  536.4 1.8 fusion.5
  538.2 0.0 copy-done.7
  538.2 0.0 copy-start.6
  538.2 0.8 fusion.20
  539.0 0.2 copy-done.6
  539.2 0.8 convolution_add_fusion
  540.1 1.8 fusion.12
  541.9 2.1 copy.38
  544.0 0.0 reduce-scatter.4.cloned.1.call-update
  544.0 1.6 copy_bitcast_fusion.6
  545.7 2.3 gather_fusion.5
  548.0 0.0 copy-start.4
  548.0 1.5 fusion.32
  549.5 0.0 copy-done.4
  549.5 0.5 fusion.33
  550.1 1.3 convolution_convert_fusion.1
  551.4 0.0 copy-start.3
  551.4 0.0 copy-start.5
  551.4 1.3 convolution_convert_fusion.2
  552.7 1.0 copy.64
  553.6 1.0 copy.65
  554.6 0.0 copy-done.3
  554.6 0.0 copy-done.5
  554.6 0.6 fusion.14
  555.2 1.2 convolution_convert_fusion
  556.4 1.0 copy.63
  557.4 29.0 %reduce-scatter.4.cloned.1.call-done = f32[160,64]{1,0:T(8,128)} async-done(((f32[1280,64]{1,0:T(8,128)}), f32[160,64]{1,0:T(8,128)}) %reduce-scatter.4.cloned.1.call-update) | async-done | bytes 40976
  586.4 1.6 copy.37
  (14 shorter events, 0.1 us)
Async XLA Ops:
  7.2 4.3 copy-start
  7.2 579.2 %reduce-scatter.4.cloned.1.call-start = ((), (), s32[]{:S(2)}) async-start(), calls=%async_computation.1 | async-start | bytes 737280
  12.2 2.5 copy-start.2
  14.7 517.5 %copy-start.8 = (bf16[64,3584]{1,0:T(8,128)(2,1)S(1)}, bf16[64,3584]{1,0:T(8,128)(2,1)}, u32[]{:S(2)}) copy-start(bf16[64,3584]{1,0:T(8,128)(2,1)} %param.16) | copy-start | bytes 1376260
  532.2 4.1 copy-start.1
  536.3 1.8 copy-start.7
  538.2 1.0 copy-start.6
  548.0 1.5 copy-start.4
  551.4 3.2 copy-start.3
  551.4 3.2 copy-start.5
Sparse Core Ops, SparseCore 0:
  544.2 42.1 reduce-scatter.3
where the time goes:
time: 599 us; the launch traced here: 595 us
  blocking collectives  517 us (86%)
  waiting for transfers between devices  29 us (5%)
  local copies, waits for them, and re-layouts  19 us (3%)
  between operations  14.3 us (2%)
  matrix products  11.8 us (2%)
    psum x1, blocking collectives, shards(): grad_hidden = lax.psum(hidden_terms, 'dp').astype(jnp.bfloat16)  517 us
    unnamed x2, waiting for transfers between devices  29 us
  transfers between devices with their start and end apart: 1, of which 1 were waited for; matrix products, arithmetic and copies ran while one was open for 2% of the time, Pallas kernels for 0%

commit v1 on v0

v1 whole, which is shorter than its diff:
```python
import functools

import jax
import jax.numpy as jnp
from jax import lax
from jax.experimental import pallas as pl
from jax.experimental.pallas import tpu as pltpu
from jax.sharding import PartitionSpec as P

MESH = pl.DeviceIdType.MESH
BF16 = jnp.bfloat16
F32 = jnp.float32

WIDTH = 64
TILES = 10
TILE = 128
BLOCK = 128
KMAX = 24
PER = 3
PAIRS = TILES * PER
OWN = 28
HALF_PAIRS = PAIRS // 2
HALF_TILES = TILES // 2
HALF = HALF_PAIRS * TILE
PART_ROWS = WIDTH + 16
VMEM_LIMIT = 24 * 1024 * 1024


def sizes(side):
    chunk = HALF // side
    return chunk, -(-chunk // side // 16) * 16


def rows_of(ref, half, place, chunk, stride):
    first = place * TILE
    parts = []
    left = TILE
    while left:
        number, offset = divmod(first, chunk)
        take = min(left, chunk - offset)
        start = number * stride + offset
        parts.append(ref[half, start : start + take, :])
        first += take
        left -= take
    return parts[0] if len(parts) == 1 else jnp.concatenate(parts, axis=0)


def terms_kernel(ids, counts, go, down, own, half_send, places):
    core = lax.rem(lax.axis_index("dp"), 2)
    low = lax.axis_index("blk") * OWN

    def scan_tile(t, first):
        live = counts[t]
        packed = jnp.int32(0)
        scale = jnp.int32(1)
        number = jnp.int32(0)
        for k in range(KMAX):
            block = ids[t, k] - low
            owned = (block >= 0) & (block < OWN) & (live > k)
            packed = packed + jnp.where(owned, (block + 1) * scale, 0)
            scale = jnp.where(owned, scale * 32, scale)
            number = number + jnp.where(owned, 1, 0)
        for j in range(PER):
            places[t * PER + j] = lax.shift_right_logical(packed, jnp.int32(5 * j)) & 31
            places[PAIRS + t * PER + j] = jnp.minimum(first + j, PAIRS - 1)
        return first + number

    lax.fori_loop(0, TILES, scan_tile, jnp.int32(0))

    def hidden_terms(t):
        tokens = go[:, pl.ds(pl.multiple_of(t * TILE, TILE), TILE)]
        blocks = []
        for j in range(PER):
            block = jnp.maximum(places[t * PER + j] - 1, 0)
            blocks.append(down[:, pl.ds(pl.multiple_of(block * BLOCK, BLOCK), BLOCK)])
        weights = jnp.concatenate(blocks, axis=1)
        return lax.dot_general(
            tokens, weights, (((0,), (0,)), ((), ())), preferred_element_type=F32
        )

    for i in range(HALF_TILES):
        others = hidden_terms((1 - core) * HALF_TILES + i)
        mine = hidden_terms(core * HALF_TILES + i)
        for j in range(PER):
            start = (i * PER + j) * TILE
            columns = slice(j * BLOCK, (j + 1) * BLOCK)
            half_send[start : start + TILE, :] = others[:, columns].astype(BF16)
            own[start : start + TILE, :] = mine[:, columns]


def sum_kernel(
    side,
    own_hbm,
    half_send,
    gh,
    own,
    half_recv,
    a_send,
    a_recv,
    b_send,
    b_recv,
    load_sem,
    h_ssem,
    h_rsem,
    a_ssem,
    a_rsem,
    b_ssem,
    b_rsem,
    c_ssem,
    c_rsem,
    d_ssem,
    d_rsem,
    f_ssem,
    f_rsem,
):
    chunk, piece = sizes(side)
    stride = piece * side
    dp = lax.axis_index("dp")
    me_z = lax.axis_index("blk")
    core = dp % 2
    me_y = (dp // 2) % side
    me_x = dp // (2 * side)
    partner = dp + 1 - 2 * core
    me_a = me_x + core * (me_y - me_x)
    me_b = me_y + core * (me_x - me_y)
    step_a = (1 - core) * 2 * side + core * 2
    step_b = (1 - core) * 2 + core * 2 * side

    def along_a(i):
        return dp + (i - me_a) * step_a

    def along_b(i):
        return dp + (i - me_b) * step_b

    def other(me, d):
        return (me + d) % side

    load = pltpu.make_async_copy(own_hbm, own, load_sem)
    load.start()

    barrier = pltpu.get_barrier_semaphore()
    pl.semaphore_signal(barrier, inc=1, device_id=(partner, me_z), device_id_type=MESH)
    for d in range(1, side):
        pl.semaphore_signal(
            barrier, inc=1, device_id=(along_a(other(me_a, d)), me_z), device_id_type=MESH
        )
        pl.semaphore_signal(
            barrier, inc=1, device_id=(along_b(other(me_b, d)), me_z), device_id_type=MESH
        )
    pl.semaphore_wait(barrier, 1 + 2 * (side - 1))

    def h_copy():
        return pltpu.make_async_remote_copy(
            src_ref=half_send,
            dst_ref=half_recv,
            send_sem=h_ssem,
            recv_sem=h_rsem,
            device_id=(partner, me_z),
            device_id_type=MESH,
        )

    h_copy().start()
    load.wait()
    h_copy().wait_recv()
    for i in range(HALF_TILES):
        rows = slice(i * PER * TILE, (i + 1) * PER * TILE)
        a_send[rows, :] = (own[rows, :] + half_recv[rows, :].astype(F32)).astype(BF16)

    def chunk_rows(i):
        return pl.ds(pl.multiple_of(i * chunk, 16), chunk)

    def a_copy(to, slot):
        return pltpu.make_async_remote_copy(
            src_ref=a_send.at[chunk_rows(to)],
            dst_ref=a_recv.at[slot],
            send_sem=a_ssem.at[to],
            recv_sem=a_rsem.at[slot],
            device_id=(along_a(to), me_z),
            device_id_type=MESH,
        )

    order = sorted(range(1, side), key=lambda d: -min(d, side - d))
    for d in order:
        a_copy(other(me_a, d), me_a).start()
    total = a_send[chunk_rows(me_a), :].astype(F32)
    for d in reversed(order):
        source = other(me_a, d)
        a_copy(source, source).wait_recv()
        total = total + a_recv[source].astype(F32)
    b_send[0:chunk, :] = total.astype(BF16)
    if stride > chunk:
        b_send[chunk:stride, :] = jnp.zeros((stride - chunk, BLOCK), BF16)

    def piece_rows(i):
        return pl.ds(pl.multiple_of(i * piece, 16), piece)

    def b_copy(to, slot):
        return pltpu.make_async_remote_copy(
            src_ref=b_send.at[piece_rows(to)],
            dst_ref=b_recv.at[slot],
            send_sem=b_ssem.at[to],
            recv_sem=b_rsem.at[slot],
            device_id=(along_b(to), me_z),
            device_id_type=MESH,
        )

    for d in order:
        b_copy(other(me_b, d), me_b).start()
    total = b_send[piece_rows(me_b), :].astype(F32)
    for d in reversed(order):
        source = other(me_b, d)
        b_copy(source, source).wait_recv()
        total = total + b_recv[source].astype(F32)

    def c_copy(to, slot):
        rows = pl.ds(pl.multiple_of(me_a * stride + slot * piece, 16), piece)
        return pltpu.make_async_remote_copy(
            src_ref=gh.at[core, rows],
            dst_ref=gh.at[core, rows],
            send_sem=c_ssem.at[to],
            recv_sem=c_rsem.at[slot],
            device_id=(along_b(to), me_z),
            device_id_type=MESH,
        )

    def d_copy(to, slot):
        rows = pl.ds(pl.multiple_of(slot * stride, 16), chunk)
        return pltpu.make_async_remote_copy(
            src_ref=gh.at[core, rows],
            dst_ref=gh.at[core, rows],
            send_sem=d_ssem.at[to],
            recv_sem=d_rsem.at[slot],
            device_id=(along_a(to), me_z),
            device_id_type=MESH,
        )

    def f_copy(slot, half):
        rows = pl.ds(pl.multiple_of(slot * stride, 16), chunk)
        return pltpu.make_async_remote_copy(
            src_ref=gh.at[half, rows],
            dst_ref=gh.at[half, rows],
            send_sem=f_ssem.at[slot],
            recv_sem=f_rsem.at[slot],
            device_id=(partner, me_z),
            device_id_type=MESH,
        )

    rows = pl.ds(pl.multiple_of(me_a * stride + me_b * piece, 16), piece)
    gh[core, rows, :] = total.astype(BF16)
    for d in order:
        c_copy(other(me_b, d), me_b).start()
    for d in reversed(order):
        source = other(me_b, d)
        c_copy(source, source).wait_recv()
    for d in order:
        d_copy(other(me_a, d), me_a).start()
    f_copy(me_a, core).start()
    for d in reversed(order):
        source = other(me_a, d)
        d_copy(source, source).wait_recv()
        f_copy(source, core).start()
    for d in range(side):
        f_copy(d, 1 - core).wait_recv()

    h_copy().wait_send()
    for d in range(1, side):
        a_copy(other(me_a, d), me_a).wait_send()
        b_copy(other(me_b, d), me_b).wait_send()
        c_copy(other(me_b, d), me_b).wait_send()
        d_copy(other(me_a, d), me_a).wait_send()
    for d in range(side):
        f_copy(d, core).wait_send()


def grads_kernel(
    side,
    depth,
    places,
    gh,
    go,
    inp,
    up,
    gate,
    sg,
    su,
    up_out,
    gate_out,
    down_out,
    parts,
    totals,
    gx,
):
    chunk, piece = sizes(side)
    stride = piece * side
    totals[...] = jnp.zeros_like(totals)
    for t in range(TILES):
        half, i = divmod(t, HALF_TILES)
        weights = []
        values = []
        tokens = slice(t * TILE, (t + 1) * TILE)
        for j in range(PER):
            number = t * PER + j
            place = places[number]
            slot = places[PAIRS + number]
            live = jnp.where(place > 0, jnp.float32(1), jnp.float32(0))
            block = jnp.maximum(place - 1, 0)
            gate_value = sg[slot].astype(F32)
            up_value = su[slot].astype(F32)
            positive = jnp.maximum(gate_value, 0.0) * live
            value = rows_of(gh, half, i * PER + j, chunk, stride).astype(F32)
            hidden = (positive * up_value).astype(BF16)
            grad_up = (value * positive).astype(BF16)
            grad_gate = (value * (jnp.where(gate_value > 0, up_value, 0.0) * live)).astype(BF16)
            columns = pl.ds(pl.multiple_of(block * BLOCK, BLOCK), BLOCK)
            weights += [up[:, columns], gate[:, columns]]
            values += [grad_up, grad_gate]
            pair = jnp.dot(
                inp[:, tokens],
                jnp.concatenate([grad_up, grad_gate], axis=1),
                preferred_element_type=F32,
            )
            totals[0, block] += pair[:, 0:BLOCK]
            totals[1, block] += pair[:, BLOCK : 2 * BLOCK]
            totals[2, block] += jnp.dot(go[:, tokens], hidden, preferred_element_type=F32)
        gx[t] = lax.dot_general(
            jnp.concatenate(weights, axis=1),
            jnp.concatenate(values, axis=1),
            (((1,), (1,)), ((), ())),
            preferred_element_type=F32,
        )
    for i, out in enumerate((up_out, gate_out, down_out)):
        for b in range(OWN):
            out[:, b * BLOCK : (b + 1) * BLOCK] = totals[i, b].astype(BF16)

    lanes = lax.broadcasted_iota(jnp.int32, (WIDTH, TILE), 1)
    short = lax.broadcasted_iota(jnp.int32, (16, TILE), 1)
    for to in range(depth):
        q, o = divmod(to * TILES * TILE // depth, TILE)
        after = gx[q + 1]
        if o:
            first = jnp.where(
                lanes < TILE - o,
                pltpu.roll(gx[q], TILE - o, 1),
                pltpu.roll(after, TILE - o, 1),
            )
        else:
            first = gx[q]
        parts[to, 0:WIDTH, :] = first.astype(BF16)
        rest = jnp.zeros((16, TILE), F32)
        for s in range(4):
            shift = (32 * s - o) % TILE
            moved = after[16 * s : 16 * (s + 1), :]
            if shift:
                moved = pltpu.roll(moved, shift, 1)
            rest = jnp.where(short // 32 == s, moved, rest)
        parts[to, WIDTH:PART_ROWS, :] = rest.astype(BF16)


def parts_kernel(depth, parts, gx_out, own, recv, load_sem, ssem, rsem):
    dp = lax.axis_index("dp")
    me_z = lax.axis_index("blk")
    load = pltpu.make_async_copy(parts.at[me_z], own, load_sem)
    load.start()

    def other(d):
        return (me_z + d) % depth

    barrier = pltpu.get_barrier_semaphore()
    for d in range(1, depth):
        pl.semaphore_signal(barrier, inc=1, device_id=(dp, other(d)), device_id_type=MESH)
    pl.semaphore_wait(barrier, depth - 1)

    def z_copy(to, slot):
        return pltpu.make_async_remote_copy(
            src_ref=parts.at[to],
            dst_ref=recv.at[slot],
            send_sem=ssem.at[to],
            recv_sem=rsem.at[slot],
            device_id=(dp, to),
            device_id_type=MESH,
        )

    order = sorted(range(1, depth), key=lambda d: -min(d, depth - d))
    for d in order:
        z_copy(other(d), me_z).start()
    load.wait()
    total = own[...].astype(F32)
    for d in reversed(order):
        source = other(d)
        z_copy(source, source).wait_recv()
        total = total + recv[source].astype(F32)
    gx_out[:, 0:TILE] = total[0:WIDTH, :].astype(BF16)
    rest = total[WIDTH:PART_ROWS, :]
    for s in range(4):
        moved = pltpu.roll(rest, TILE - 32 * s, 1) if s else rest
        gx_out[16 * s : 16 * (s + 1), TILE : TILE + 32] = moved[:, 0:32].astype(BF16)
    for d in range(1, depth):
        z_copy(other(d), me_z).wait_send()


def shards(
    side,
    depth,
    inputs,
    grad_out,
    up_weight,
    gate_weight,
    down_weight,
    saved_gate,
    saved_up,
    block_ids,
    counts,
):
    tokens = TILES * TILE
    units = OWN * BLOCK
    chunk, piece = sizes(side)
    stride = piece * side
    dma = pltpu.SemaphoreType.DMA
    anywhere = pl.BlockSpec(memory_space=pl.ANY)
    smem = pl.BlockSpec(memory_space=pltpu.SMEM)
    vmem = pl.BlockSpec(memory_space=pltpu.VMEM)
    go = grad_out.T
    shape = jax.ShapeDtypeStruct
    own, half_send, places = pl.pallas_call(
        terms_kernel,
        out_shape=[
            shape((HALF, BLOCK), F32),
            shape((HALF, BLOCK), BF16),
            shape((2 * PAIRS,), jnp.int32),
        ],
        in_specs=[smem, smem, vmem, vmem],
        out_specs=[vmem, vmem, smem],
        compiler_params=pltpu.CompilerParams(vmem_limit_bytes=VMEM_LIMIT),
    )(block_ids, counts, go, down_weight.T)
    gh = pl.pallas_call(
        functools.partial(sum_kernel, side),
        out_shape=shape((2, side * stride, BLOCK), BF16),
        in_specs=[anywhere, anywhere],
        out_specs=vmem,
        scratch_shapes=[
            pltpu.VMEM((HALF, BLOCK), F32),
            pltpu.VMEM((HALF, BLOCK), BF16),
            pltpu.VMEM((HALF, BLOCK), BF16),
            pltpu.VMEM((side, chunk, BLOCK), BF16),
            pltpu.VMEM((stride, BLOCK), BF16),
            pltpu.VMEM((side, piece, BLOCK), BF16),
            dma,
            dma,
            dma,
        ]
        + [dma((side,))] * 10,
        compiler_params=pltpu.CompilerParams(
            collective_id=0, has_side_effects=True, vmem_limit_bytes=VMEM_LIMIT
        ),
    )(own, half_send)
    grad_up, grad_gate, grad_down, parts = pl.pallas_call(
        functools.partial(grads_kernel, side, depth),
        out_shape=[shape((WIDTH, units), BF16)] * 3
        + [shape((depth, PART_ROWS, TILE), BF16)],
        in_specs=[smem] + [vmem] * 7,
        out_specs=[vmem] * 4,
        scratch_shapes=[
            pltpu.VMEM((3, OWN, WIDTH, BLOCK), F32),
            pltpu.VMEM((TILES, WIDTH, TILE), F32),
        ],
        compiler_params=pltpu.CompilerParams(vmem_limit_bytes=VMEM_LIMIT),
    )(places, gh, go, inputs.T, up_weight, gate_weight, saved_gate[0], saved_up[0])
    grad_x = pl.pallas_call(
        functools.partial(parts_kernel, depth),
        out_shape=shape((WIDTH, tokens // depth), BF16),
        in_specs=[anywhere],
        out_specs=vmem,
        scratch_shapes=[
            pltpu.VMEM((PART_ROWS, TILE), BF16),
            pltpu.VMEM((depth, PART_ROWS, TILE), BF16),
            dma,
            dma((depth,)),
            dma((depth,)),
        ],
        compiler_params=pltpu.CompilerParams(
            collective_id=1, has_side_effects=True, vmem_limit_bytes=VMEM_LIMIT
        ),
    )(parts)
    return (grad_x.T, grad_up, grad_gate, grad_down.T)


def solution(mesh):
    side = 1
    while 2 * side * side < mesh.shape["dp"]:
        side += 1
    in_specs = (
        P(None, "dp"),
        P(None, "dp"),
        P("dp", "blk"),
        P("dp", "blk"),
        P("blk", "dp"),
        P("blk", None, None, None),
        P("blk", None, None, None),
        P(),
        P(),
    )
    out_specs = (P("blk", "dp"), P("dp", "blk"), P("dp", "blk"), P("blk", "dp"))
    return jax.shard_map(
        functools.partial(shards, side, mesh.shape["blk"]),
        mesh=mesh,
        in_specs=in_specs,
        out_specs=out_specs,
        check_vma=False,
    )
```

time: 599 us -> 72.4 us (0.12)
  blocking collectives: 517 us -> 0 us
  Pallas kernels: 0 us -> 67.1 us
  waiting for transfers between devices: 29 us -> 0 us
  local copies, waits for them, and re-layouts: 19 us -> 4.17 us
  between operations: 14.3 us -> 0.75 us
  matrix products: 11.8 us -> 0 us
    psum x1 -> x0, blocking collectives: 517 us -> none  [shards(): grad_hidden = lax.psum(hidden_terms, 'dp').astype(jnp.bfloat16)]
    pallas_call x0 -> x4, Pallas kernels: none -> 67.1 us  [the longest x1 46.1 us: shards(): pl.pallas_call(functools.partial(sum_kernel, side), out_shape=shape((2, s...]
    unnamed x2 -> x0, waiting for transfers between devices: 29 us -> none
    dot_general x10 -> x0, matrix products: 11.8 us -> none  [the longest x1 1.83 us: shards(): jnp.einsum('std,sbd->stb', grad_slots, down_slots, preferred_element_type...]
    gather x6 -> x0, local copies, waits for them, and re-layouts: 7.07 us -> none  [the longest x1 2.3 us: shards(): jnp.take(inputs.reshape(tile_count, tile_len, model_width), tile_of, axis=0)]
  transfers between devices with their start and end apart: 1 -> 0, of which waited for: 1 -> 0; matrix products, arithmetic and copies ran while one was open for 2% -> 0% of each run, Pallas kernels for 0% -> 0%
where the time goes in v1:
time: 72.4 us; the launch traced here: 72 us
  Pallas kernels  67.1 us (93%)
  local copies, waits for them, and re-layouts  4.17 us (6%)
  between operations  0.75 us (1%)
    pallas_call x1, Pallas kernels, shards(): pl.pallas_call(functools.partial(sum_kernel, side), out_shape=shape((2, s...  46.1 us
    pallas_call x1, Pallas kernels, shards(): pl.pallas_call(functools.partial(parts_kernel, depth), out_shape=shape((W...  15.1 us
    unnamed x21, local copies, waits for them, and re-layouts  4.17 us
    pallas_call x1, Pallas kernels, shards(): pl.pallas_call(functools.partial(grads_kernel, side, depth), out_shape=[s...  3.1 us
    pallas_call x1, Pallas kernels, shards(): pl.pallas_call(terms_kernel, out_shape=[shape((HALF, BLOCK), F32), shape(...  2.79 us

profile of v1, /device:TPU:1, one launch (start us, length us, event | category | flops | bytes accessed | tf_op | source)
XLA Modules:
  0.0 72.0 jit_solution(3975947583555163983)
XLA Ops:
  0.6 0.0 copy-start.8
  0.6 0.0 copy-start.9
  0.7 0.7 copy-done.8
  1.3 0.0 copy-done.9
  1.3 0.0 copy-start.2
  1.3 0.9 %copy-done.2 = bf16[1280,64]{0,1:T(8,128)(2,1)S(1)} copy-done((bf16[1280,64]{0,1:T(8,128)(2,1)S(1)}, bf16[1280,64]{0,1:T(8,128)(2,1)}, u32[]{:S(2)}) %copy-start.2) | copy-done | bytes 163864
  2.2 0.0 copy-start.6
  2.3 1.0 %copy-done.6 = bf16[3584,64]{0,1:T(8,128)(2,1)S(1)} copy-done((bf16[3584,64]{0,1:T(8,128)(2,1)S(1)}, bf16[3584,64]{0,1:T(8,128)(2,1)}, u32[]{:S(2)}) %copy-start.6) | copy-done | bytes 458776
  3.3 0.0 copy-start.4
  3.3 0.0 copy-start.5
  3.3 2.8 %shard_map.120 = (f32[1920,128]{1,0:T(8,128)S(1)}, bf16[1920,128]{1,0:T(8,128)(2,1)S(1)}, s32[60]{0:T(128)S(1)}) custom-call(s32[10,24]{1,0:T(8,128)S(1)} %copy-done.8, s32[10]{0:T(128)S(1)} %copy-done.9, bf16[64,1280]{1,0:T(8,128)(2,1)S(1)} %bitcast.9, bf16[64,3584]{1,0:T(8,128)(2,1)S(1)} %bitcast.11), custom_call_target="tpu_custom_call" | custom-call | tf_op jit(solution)/shard_map/pallas_call | solution.py:424
  6.1 0.0 copy-start
  6.1 0.0 copy-start.1
  6.1 0.0 copy-start.3
  6.1 46.1 %shard_map.121.gh = bf16[2,2048,128]{2,1,0:T(8,128)(2,1)S(1)} custom-call(f32[1920,128]{1,0:T(8,128)S(1)} %get-tuple-element.12.own_hbm, bf16[1920,128]{1,0:T(8,128)(2,1)S(1)} %get-tuple-element.13.half_send), custom_call_target="tpu_custom_call" | custom-call | tf_op jit(solution)/shard_map/pallas_call | solution.py:435
  52.2 0.0 copy-done.4
  52.2 0.0 copy-done.5
  52.2 0.0 copy-done
  52.2 0.0 copy-done.1
  52.2 0.0 copy-done.3
  52.2 0.0 copy-start.7
  52.2 0.9 %copy-done.7 = bf16[1280,64]{0,1:T(8,128)(2,1)S(1)} copy-done((bf16[1280,64]{0,1:T(8,128)(2,1)S(1)}, bf16[1280,64]{0,1:T(8,128)(2,1)}, u32[]{:S(2)}) %copy-start.7) | copy-done | bytes 163864
  53.2 3.1 %shard_map.122 = (bf16[64,3584]{1,0:T(8,128)(2,1)}, bf16[64,3584]{1,0:T(8,128)(2,1)}, bf16[64,3584]{1,0:T(8,128)(2,1)}, bf16[8,80,128]{2,1,0:T(8,128)(2,1)S(1)}) custom-call(s32[60]{0:T(128)S(1)} %get-tuple-element.11.places, bf16[2,2048,128]{2,1,0:T(8,128)(2,1)S(1)} %shard_map.121.gh, bf16[64,1280]{1,0:T(8,128)(2,1)S(1)} %bitcast.10, ...), custom_call_target="tpu_custom_call" | custom-call | tf_op jit(solution)/shard_map/pallas_call | solution.py:456
  56.3 15.1 %shard_map.123 = bf16[64,160]{1,0:T(8,128)(2,1)S(1)} custom-call(bf16[8,80,128]{2,1,0:T(8,128)(2,1)S(1)} %get-tuple-element.14.parts), custom_call_target="tpu_custom_call" | custom-call | tf_op jit(solution)/shard_map/pallas_call | solution.py:468
  71.4 0.6 copy.14
Async XLA Ops:
  0.6 0.7 copy-start.8
  0.6 0.7 copy-start.9
  1.3 0.9 %copy-start.2 = (bf16[1280,64]{0,1:T(8,128)(2,1)S(1)}, bf16[1280,64]{0,1:T(8,128)(2,1)}, u32[]{:S(2)}) copy-start(bf16[1280,64]{0,1:T(8,128)(2,1)} %param.10) | copy-start | bytes 491524
  2.2 1.0 %copy-start.6 = (bf16[3584,64]{0,1:T(8,128)(2,1)S(1)}, bf16[3584,64]{0,1:T(8,128)(2,1)}, u32[]{:S(2)}) copy-start(bf16[3584,64]{0,1:T(8,128)(2,1)} %param.13) | copy-start | bytes 1376260
  3.3 48.9 %copy-start.4 = (bf16[64,3584]{1,0:T(8,128)(2,1)S(1)}, bf16[64,3584]{1,0:T(8,128)(2,1)}, u32[]{:S(2)}) copy-start(bf16[64,3584]{1,0:T(8,128)(2,1)} %up.1) | copy-start | bytes 1376260
  3.3 48.9 %copy-start.5 = (bf16[64,3584]{1,0:T(8,128)(2,1)S(1)}, bf16[64,3584]{1,0:T(8,128)(2,1)}, u32[]{:S(2)}) copy-start(bf16[64,3584]{1,0:T(8,128)(2,1)} %gate.1) | copy-start | bytes 1376260
  6.1 46.1 %copy-start = (bf16[1,30,128,128]{3,2,1,0:T(8,128)(2,1)S(1)}, bf16[1,30,128,128]{3,2,1,0:T(8,128)(2,1)}, u32[]{:S(2)}) copy-start(bf16[1,30,128,128]{3,2,1,0:T(8,128)(2,1)} %param.14) | copy-start | bytes 2949124
  6.1 46.1 %copy-start.1 = (bf16[1,30,128,128]{3,2,1,0:T(8,128)(2,1)S(1)}, bf16[1,30,128,128]{3,2,1,0:T(8,128)(2,1)}, u32[]{:S(2)}) copy-start(bf16[1,30,128,128]{3,2,1,0:T(8,128)(2,1)} %param.15) | copy-start | bytes 2949124
  6.1 46.1 %copy-start.3 = (bf16[1280,64]{0,1:T(8,128)(2,1)S(1)}, bf16[1280,64]{0,1:T(8,128)(2,1)}, u32[]{:S(2)}) copy-start(bf16[1280,64]{0,1:T(8,128)(2,1)} %param.10) | copy-start | bytes 491524
  52.2 0.9 %copy-start.7 = (bf16[1280,64]{0,1:T(8,128)(2,1)S(1)}, bf16[1280,64]{0,1:T(8,128)(2,1)}, u32[]{:S(2)}) copy-start(bf16[1280,64]{0,1:T(8,128)(2,1)} %param.9) | copy-start | bytes 491524

commit v2 on v1

--- a/solution.py
+++ b/solution.py
@@ -26,9 +26,24 @@
 VMEM_LIMIT = 24 * 1024 * 1024
 
 
+EARLY = 1
+SUBS = 2
+
+
 def sizes(side):
     chunk = HALF // side
-    return chunk, -(-chunk // side // 16) * 16
+    subs = []
+    offset = 0
+    for n in range(SUBS):
+        number = min(-(-chunk // (SUBS * 16 * side)) * 16 * side, chunk - offset)
+        piece = -(-number // side // 16) * 16
+        subs.append((offset, number, piece))
+        offset += number
+    return chunk, subs
+
+
+def stride_of(side):
+    return sum(piece for _, _, piece in sizes(side)[1]) * side
 
 
 def rows_of(ref, half, place, chunk, stride):
@@ -45,55 +60,54 @@
     return parts[0] if len(parts) == 1 else jnp.concatenate(parts, axis=0)
 
 
-def terms_kernel(ids, counts, go, down, own, half_send, places):
-    core = lax.rem(lax.axis_index("dp"), 2)
+def pick_kernel(ids, counts, down_hbm, picked, places, down, load_sem):
+    load = pltpu.make_async_copy(down_hbm, down, load_sem)
+    load.start()
     low = lax.axis_index("blk") * OWN
 
-    def scan_tile(t, first):
+    first = jnp.int32(0)
+    for t in range(TILES):
         live = counts[t]
         packed = jnp.int32(0)
-        scale = jnp.int32(1)
-        number = jnp.int32(0)
+        shift = jnp.int32(0)
         for k in range(KMAX):
             block = ids[t, k] - low
             owned = (block >= 0) & (block < OWN) & (live > k)
-            packed = packed + jnp.where(owned, (block + 1) * scale, 0)
-            scale = jnp.where(owned, scale * 32, scale)
-            number = number + jnp.where(owned, 1, 0)
+            packed = packed + jnp.where(owned, lax.shift_left(block + 1, shift), 0)
+            shift = shift + jnp.where(owned, 5, 0)
+        number = jnp.int32(0)
         for j in range(PER):
-            places[t * PER + j] = lax.shift_right_logical(packed, jnp.int32(5 * j)) & 31
+            place = lax.shift_right_logical(packed, jnp.int32(5 * j)) & 31
+            places[t * PER + j] = place
             places[PAIRS + t * PER + j] = jnp.minimum(first + j, PAIRS - 1)
-        return first + number
-
-    lax.fori_loop(0, TILES, scan_tile, jnp.int32(0))
-
-    def hidden_terms(t):
-        tokens = go[:, pl.ds(pl.multiple_of(t * TILE, TILE), TILE)]
-        blocks = []
+            number = number + jnp.where(place > 0, 1, 0)
+        first = first + number
+
+    load.wait()
+    for t in range(TILES):
         for j in range(PER):
             block = jnp.maximum(places[t * PER + j] - 1, 0)
-            blocks.append(down[:, pl.ds(pl.multiple_of(block * BLOCK, BLOCK), BLOCK)])
-        weights = jnp.concatenate(blocks, axis=1)
-        return lax.dot_general(
-            tokens, weights, (((0,), (0,)), ((), ())), preferred_element_type=F32
-        )
-
-    for i in range(HALF_TILES):
-        others = hidden_terms((1 - core) * HALF_TILES + i)
-        mine = hidden_terms(core * HALF_TILES + i)
-        for j in range(PER):
-            start = (i * PER + j) * TILE
-            columns = slice(j * BLOCK, (j + 1) * BLOCK)
-            half_send[start : start + TILE, :] = others[:, columns].astype(BF16)
-            own[start : start + TILE, :] = mine[:, columns]
+            columns = pl.ds(pl.multiple_of(block * BLOCK, BLOCK), BLOCK)
+            picked[t, :, j * BLOCK : (j + 1) * BLOCK] = down[:, columns]
 
 
 def sum_kernel(
     side,
-    own_hbm,
+    go,
+    picked,
+    inp_hbm,
+    up_hbm,
+    gate_hbm,
+    sg_hbm,
+    su_hbm,
+    gh,
+    inp,
+    up,
+    gate,
+    sg,
+    su,
+    own,
     half_send,
-    gh,
-    own,
     half_recv,
     a_send,
     a_recv,
@@ -113,8 +127,8 @@
     f_ssem,
     f_rsem,
 ):
-    chunk, piece = sizes(side)
-    stride = piece * side
+    chunk, subs = sizes(side)
+    stride = stride_of(side)
     dp = lax.axis_index("dp")
     me_z = lax.axis_index("blk")
     core = dp % 2
@@ -135,9 +149,6 @@
     def other(me, d):
         return (me + d) % side
 
-    load = pltpu.make_async_copy(own_hbm, own, load_sem)
-    load.start()
-
     barrier = pltpu.get_barrier_semaphore()
     pl.semaphore_signal(barrier, inc=1, device_id=(partner, me_z), device_id_type=MESH)
     for d in range(1, side):
@@ -147,129 +158,170 @@
         pl.semaphore_signal(
             barrier, inc=1, device_id=(along_b(other(me_b, d)), me_z), device_id_type=MESH
         )
-    pl.semaphore_wait(barrier, 1 + 2 * (side - 1))
-
-    def h_copy():
-        return pltpu.make_async_remote_copy(
-            src_ref=half_send,
-            dst_ref=half_recv,
-            send_sem=h_ssem,
-            recv_sem=h_rsem,
+
+    loads = [
+        pltpu.make_async_copy(source, target, load_sem.at[i])
+        for i, (source, target) in enumerate(
+            ((inp_hbm, inp), (up_hbm, up), (gate_hbm, gate), (sg_hbm, sg), (su_hbm, su))
+        )
+    ]
+    for load in loads:
+        load.start()
+
+    def hidden_terms(t):
+        tokens = go[:, pl.ds(pl.multiple_of(t * TILE, TILE), TILE)]
+        return lax.dot_general(
+            tokens, picked[t], (((0,), (0,)), ((), ())), preferred_element_type=F32
+        )
+
+    def h_copy(i):
+        rows = pl.ds(i * PER * TILE, PER * TILE)
+        return pltpu.make_async_remote_copy(
+            src_ref=half_send.at[rows],
+            dst_ref=half_recv.at[rows],
+            send_sem=h_ssem.at[i],
+            recv_sem=h_rsem.at[i],
             device_id=(partner, me_z),
             device_id_type=MESH,
         )
 
-    h_copy().start()
-    load.wait()
-    h_copy().wait_recv()
     for i in range(HALF_TILES):
+        others = hidden_terms((1 - core) * HALF_TILES + i)
+        for j in range(PER):
+            start = (i * PER + j) * TILE
+            half_send[start : start + TILE, :] = others[:, j * BLOCK : (j + 1) * BLOCK].astype(BF16)
+    for i in range(HALF_TILES):
+        mine = hidden_terms(core * HALF_TILES + i)
+        for j in range(PER):
+            start = (i * PER + j) * TILE
+            own[start : start + TILE, :] = mine[:, j * BLOCK : (j + 1) * BLOCK]
+        if i == EARLY:
+            pl.semaphore_wait(barrier, 1 + 2 * (side - 1))
+            for k in range(HALF_TILES):
+                h_copy(k).start()
+    for i in range(HALF_TILES):
+        h_copy(i).wait_recv()
         rows = slice(i * PER * TILE, (i + 1) * PER * TILE)
         a_send[rows, :] = (own[rows, :] + half_recv[rows, :].astype(F32)).astype(BF16)
 
-    def chunk_rows(i):
-        return pl.ds(pl.multiple_of(i * chunk, 16), chunk)
-
-    def a_copy(to, slot):
-        return pltpu.make_async_remote_copy(
-            src_ref=a_send.at[chunk_rows(to)],
-            dst_ref=a_recv.at[slot],
-            send_sem=a_ssem.at[to],
-            recv_sem=a_rsem.at[slot],
+    def a_copy(to, slot, n):
+        offset, number, _ = subs[n]
+        rows = pl.ds(pl.multiple_of(to * chunk + offset, 16), number)
+        return pltpu.make_async_remote_copy(
+            src_ref=a_send.at[rows],
+            dst_ref=a_recv.at[slot, offset : offset + number],
+            send_sem=a_ssem.at[n, to],
+            recv_sem=a_rsem.at[n, slot],
             device_id=(along_a(to), me_z),
             device_id_type=MESH,
         )
 
-    order = sorted(range(1, side), key=lambda d: -min(d, side - d))
-    for d in order:
-        a_copy(other(me_a, d), me_a).start()
-    total = a_send[chunk_rows(me_a), :].astype(F32)
-    for d in reversed(order):
-        source = other(me_a, d)
-        a_copy(source, source).wait_recv()
-        total = total + a_recv[source].astype(F32)
-    b_send[0:chunk, :] = total.astype(BF16)
-    if stride > chunk:
-        b_send[chunk:stride, :] = jnp.zeros((stride - chunk, BLOCK), BF16)
-
-    def piece_rows(i):
-        return pl.ds(pl.multiple_of(i * piece, 16), piece)
-
-    def b_copy(to, slot):
-        return pltpu.make_async_remote_copy(
-            src_ref=b_send.at[piece_rows(to)],
-            dst_ref=b_recv.at[slot],
-            send_sem=b_ssem.at[to],
-            recv_sem=b_rsem.at[slot],
+    def b_copy(to, slot, n):
+        offset, _, piece = subs[n]
+        rows = pl.ds(pl.multiple_of(offset + to * piece, 16), piece)
+        return pltpu.make_async_remote_copy(
+            src_ref=b_send.at[rows],
+            dst_ref=b_recv.at[n, slot, 0:piece],
+            send_sem=b_ssem.at[n, to],
+            recv_sem=b_rsem.at[n, slot],
             device_id=(along_b(to), me_z),
             device_id_type=MESH,
         )
 
-    for d in order:
-        b_copy(other(me_b, d), me_b).start()
-    total = b_send[piece_rows(me_b), :].astype(F32)
-    for d in reversed(order):
-        source = other(me_b, d)
-        b_copy(source, source).wait_recv()
-        total = total + b_recv[source].astype(F32)
-
-    def c_copy(to, slot):
-        rows = pl.ds(pl.multiple_of(me_a * stride + slot * piece, 16), piece)
+    def c_copy(to, slot, n):
+        offset, _, piece = subs[n]
+        rows = pl.ds(pl.multiple_of(me_a * stride + offset + slot * piece, 16), piece)
         return pltpu.make_async_remote_copy(
             src_ref=gh.at[core, rows],
             dst_ref=gh.at[core, rows],
-            send_sem=c_ssem.at[to],
-            recv_sem=c_rsem.at[slot],
+            send_sem=c_ssem.at[n, to],
+            recv_sem=c_rsem.at[n, slot],
             device_id=(along_b(to), me_z),
             device_id_type=MESH,
         )
 
-    def d_copy(to, slot):
-        rows = pl.ds(pl.multiple_of(slot * stride, 16), chunk)
+    def d_copy(to, slot, n):
+        offset, number, _ = subs[n]
+        rows = pl.ds(pl.multiple_of(slot * stride + offset, 16), number)
         return pltpu.make_async_remote_copy(
             src_ref=gh.at[core, rows],
             dst_ref=gh.at[core, rows],
-            send_sem=d_ssem.at[to],
-            recv_sem=d_rsem.at[slot],
+            send_sem=d_ssem.at[n, to],
+            recv_sem=d_rsem.at[n, slot],
             device_id=(along_a(to), me_z),
             device_id_type=MESH,
         )
 
-    def f_copy(slot, half):
-        rows = pl.ds(pl.multiple_of(slot * stride, 16), chunk)
+    def f_copy(slot, half, n):
+        offset, number, _ = subs[n]
+        rows = pl.ds(pl.multiple_of(slot * stride + offset, 16), number)
         return pltpu.make_async_remote_copy(
             src_ref=gh.at[half, rows],
             dst_ref=gh.at[half, rows],
-            send_sem=f_ssem.at[slot],
-            recv_sem=f_rsem.at[slot],
+            send_sem=f_ssem.at[n, slot],
+            recv_sem=f_rsem.at[n, slot],
             device_id=(partner, me_z),
             device_id_type=MESH,
         )
 
-    rows = pl.ds(pl.multiple_of(me_a * stride + me_b * piece, 16), piece)
-    gh[core, rows, :] = total.astype(BF16)
-    for d in order:
-        c_copy(other(me_b, d), me_b).start()
-    for d in reversed(order):
-        source = other(me_b, d)
-        c_copy(source, source).wait_recv()
-    for d in order:
-        d_copy(other(me_a, d), me_a).start()
-    f_copy(me_a, core).start()
-    for d in reversed(order):
-        source = other(me_a, d)
-        d_copy(source, source).wait_recv()
-        f_copy(source, core).start()
-    for d in range(side):
-        f_copy(d, 1 - core).wait_recv()
-
-    h_copy().wait_send()
-    for d in range(1, side):
-        a_copy(other(me_a, d), me_a).wait_send()
-        b_copy(other(me_b, d), me_b).wait_send()
-        c_copy(other(me_b, d), me_b).wait_send()
-        d_copy(other(me_a, d), me_a).wait_send()
-    for d in range(side):
-        f_copy(d, core).wait_send()
+    order = sorted(range(1, side), key=lambda d: -min(d, side - d))
+    steps = range(len(subs))
+    for n in steps:
+        for d in order:
+            a_copy(other(me_a, d), me_a, n).start()
+    for n in steps:
+        offset, number, piece = subs[n]
+        rows = pl.ds(pl.multiple_of(me_a * chunk + offset, 16), number)
+        total = a_send[rows, :].astype(F32)
+        for d in reversed(order):
+            source = other(me_a, d)
+            a_copy(source, source, n).wait_recv()
+            total = total + a_recv[source, offset : offset + number, :].astype(F32)
+        b_send[offset : offset + number, :] = total.astype(BF16)
+        end = offset + piece * side
+        if end > offset + number:
+            b_send[offset + number : end, :] = jnp.zeros((end - offset - number, BLOCK), BF16)
+        for d in order:
+            b_copy(other(me_b, d), me_b, n).start()
+    for n in steps:
+        offset, _, piece = subs[n]
+        total = b_send[pl.ds(pl.multiple_of(offset + me_b * piece, 16), piece), :].astype(F32)
+        for d in reversed(order):
+            source = other(me_b, d)
+            b_copy(source, source, n).wait_recv()
+            total = total + b_recv[n, source, 0:piece, :].astype(F32)
+        rows = pl.ds(pl.multiple_of(me_a * stride + offset + me_b * piece, 16), piece)
+        gh[core, rows, :] = total.astype(BF16)
+        for d in order:
+            c_copy(other(me_b, d), me_b, n).start()
+    for n in steps:
+        for d in reversed(order):
+            source = other(me_b, d)
+            c_copy(source, source, n).wait_recv()
+        for d in order:
+            d_copy(other(me_a, d), me_a, n).start()
+        f_copy(me_a, core, n).start()
+    for n in steps:
+        for d in reversed(order):
+            source = other(me_a, d)
+            d_copy(source, source, n).wait_recv()
+            f_copy(source, core, n).start()
+    for n in steps:
+        for d in range(side):
+            f_copy(d, 1 - core, n).wait_recv()
+
+    for load in loads:
+        load.wait()
+    for i in range(HALF_TILES):
+        h_copy(i).wait_send()
+    for n in steps:
+        for d in range(1, side):
+            a_copy(other(me_a, d), me_a, n).wait_send()
+            b_copy(other(me_b, d), me_b, n).wait_send()
+            c_copy(other(me_b, d), me_b, n).wait_send()
+            d_copy(other(me_a, d), me_a, n).wait_send()
+        for d in range(side):
+            f_copy(d, core, n).wait_send()
 
 
 def grads_kernel(
@@ -290,8 +342,8 @@
     totals,
     gx,
 ):
-    chunk, piece = sizes(side)
-    stride = piece * side
+    chunk, _ = sizes(side)
+    stride = stride_of(side)
     totals[...] = jnp.zeros_like(totals)
     for t in range(TILES):
         half, i = divmod(t, HALF_TILES)
@@ -398,6 +450,10 @@
         z_copy(other(d), me_z).wait_send()
 
 
+def in_hbm(*arrays):
+    return [pltpu.with_memory_space_constraint(array, pltpu.HBM) for array in arrays]
+
+
 def shards(
     side,
     depth,
@@ -413,46 +469,52 @@
 ):
     tokens = TILES * TILE
     units = OWN * BLOCK
-    chunk, piece = sizes(side)
-    stride = piece * side
+    chunk, subs = sizes(side)
+    piece = max(piece for _, _, piece in subs)
+    stride = stride_of(side)
     dma = pltpu.SemaphoreType.DMA
     anywhere = pl.BlockSpec(memory_space=pl.ANY)
     smem = pl.BlockSpec(memory_space=pltpu.SMEM)
     vmem = pl.BlockSpec(memory_space=pltpu.VMEM)
     go = grad_out.T
     shape = jax.ShapeDtypeStruct
-    own, half_send, places = pl.pallas_call(
-        terms_kernel,
+    picked, places = pl.pallas_call(
+        pick_kernel,
+        out_shape=[shape((TILES, WIDTH, PER * BLOCK), BF16), shape((2 * PAIRS,), jnp.int32)],
+        in_specs=[smem, smem, anywhere],
+        out_specs=[vmem, smem],
+        scratch_shapes=[pltpu.VMEM((WIDTH, units), BF16), dma],
+        compiler_params=pltpu.CompilerParams(vmem_limit_bytes=VMEM_LIMIT),
+    )(*in_hbm(block_ids, counts, down_weight.T))
+    gh, inp, up, gate, sg, su = pl.pallas_call(
+        functools.partial(sum_kernel, side),
         out_shape=[
-            shape((HALF, BLOCK), F32),
-            shape((HALF, BLOCK), BF16),
-            shape((2 * PAIRS,), jnp.int32),
+            shape((2, side * stride, BLOCK), BF16),
+            shape((WIDTH, tokens), BF16),
+            shape((WIDTH, units), BF16),
+            shape((WIDTH, units), BF16),
+            shape((PAIRS, TILE, BLOCK), BF16),
+            shape((PAIRS, TILE, BLOCK), BF16),
         ],
-        in_specs=[smem, smem, vmem, vmem],
-        out_specs=[vmem, vmem, smem],
-        compiler_params=pltpu.CompilerParams(vmem_limit_bytes=VMEM_LIMIT),
-    )(block_ids, counts, go, down_weight.T)
-    gh = pl.pallas_call(
-        functools.partial(sum_kernel, side),
-        out_shape=shape((2, side * stride, BLOCK), BF16),
-        in_specs=[anywhere, anywhere],
-        out_specs=vmem,
+        in_specs=[vmem] * 2 + [anywhere] * 5,
+        out_specs=[vmem] * 6,
         scratch_shapes=[
             pltpu.VMEM((HALF, BLOCK), F32),
             pltpu.VMEM((HALF, BLOCK), BF16),
             pltpu.VMEM((HALF, BLOCK), BF16),
+            pltpu.VMEM((HALF, BLOCK), BF16),
             pltpu.VMEM((side, chunk, BLOCK), BF16),
             pltpu.VMEM((stride, BLOCK), BF16),
-            pltpu.VMEM((side, piece, BLOCK), BF16),
-            dma,
-            dma,
-            dma,
+            pltpu.VMEM((SUBS, side, piece, BLOCK), BF16),
+            dma((5,)),
+            dma((HALF_TILES,)),
+            dma((HALF_TILES,)),
         ]
-        + [dma((side,))] * 10,
+        + [dma((SUBS, side))] * 10,
         compiler_params=pltpu.CompilerParams(
             collective_id=0, has_side_effects=True, vmem_limit_bytes=VMEM_LIMIT
         ),
-    )(own, half_send)
+    )(go, picked, *in_hbm(inputs.T, up_weight, gate_weight, saved_gate[0], saved_up[0]))
     grad_up, grad_gate, grad_down, parts = pl.pallas_call(
         functools.partial(grads_kernel, side, depth),
         out_shape=[shape((WIDTH, units), BF16)] * 3
@@ -464,7 +526,7 @@
             pltpu.VMEM((TILES, WIDTH, TILE), F32),
         ],
         compiler_params=pltpu.CompilerParams(vmem_limit_bytes=VMEM_LIMIT),
-    )(places, gh, go, inputs.T, up_weight, gate_weight, saved_gate[0], saved_up[0])
+    )(places, gh, go, inp, up, gate, sg, su)
     grad_x = pl.pallas_call(
         functools.partial(parts_kernel, depth),
         out_shape=shape((WIDTH, tokens // depth), BF16),

time: 72.4 us -> 67.2 us (0.928)
  local copies, waits for them, and re-layouts: 4.17 us -> 0.62 us
  Pallas kernels: 67.1 us -> 65.7 us
    unnamed x21 -> x3, local copies, waits for them, and re-layouts: 4.17 us -> 0.62 us
    pallas_call x2, Pallas kernels: 48.9 us -> 47.5 us  [the longest x1 44.9 us: shards(): pl.pallas_call(functools.partial(sum_kernel, side), out_shape=[shape((2,...]
where the time goes in v2:
time: 67.2 us; the launch traced here: 67 us
  Pallas kernels  65.7 us (98%)
    pallas_call x1, Pallas kernels, shards(): pl.pallas_call(functools.partial(sum_kernel, side), out_shape=[shape((2,...  44.9 us
    pallas_call x1, Pallas kernels, shards(): pl.pallas_call(functools.partial(parts_kernel, depth), out_shape=shape((W...  15.1 us
    pallas_call x1, Pallas kernels, shards(): pl.pallas_call(functools.partial(grads_kernel, side, depth), out_shape=[s...  3.06 us
    pallas_call x1, Pallas kernels, shards(): pl.pallas_call(pick_kernel, out_shape=[shape((TILES, WIDTH, PER * BLOCK),...  2.66 us

profile of v2, /device:TPU:1, one launch (start us, length us, event | category | flops | bytes accessed | tf_op | source)
XLA Modules:
  0.0 67.0 jit_solution(5518698272012902566)
XLA Ops:
  0.6 0.0 copy-start
  0.6 2.7 %shard_map.120 = (bf16[10,64,384]{2,1,0:T(8,128)(2,1)S(1)}, s32[60]{0:T(128)S(1)}) custom-call(s32[10,24]{1,0:T(8,128)} %ids.1, s32[10]{0:T(128)} %counts.1, bf16[64,3584]{1,0:T(8,128)(2,1)} %bitcast.12), custom_call_target="tpu_custom_call" | custom-call | tf_op jit(solution)/shard_map/pallas_call | solution.py:481
  3.3 0.0 copy-done
  3.3 44.9 %shard_map.121 = (bf16[2,2048,128]{2,1,0:T(8,128)(2,1)S(1)}, bf16[64,1280]{1,0:T(8,128)(2,1)S(1)}, bf16[64,3584]{1,0:T(8,128)(2,1)S(1)}, bf16[64,3584]{1,0:T(8,1...) custom-call(bf16[64,1280]{1,0:T(8,128)(2,1)S(1)} %bitcast.7, ...), custom_call_target="tpu_custom_call" | custom-call | tf_op jit(solution)/shard_map/pallas_call | solution.py:489
  48.2 3.1 %shard_map.122 = (bf16[64,3584]{1,0:T(8,128)(2,1)}, bf16[64,3584]{1,0:T(8,128)(2,1)}, bf16[64,3584]{1,0:T(8,128)(2,1)}, bf16[8,80,128]{2,1,0:T(8,128)(2,1)S(1)}) custom-call(s32[60]{0:T(128)S(1)} %get-tuple-element.16.places, bf16[2,2048,128]{2,1,0:T(8,128)(2,1)S(1)} %get-tuple-element.18.gh, bf16[64,1280]{1,0:T(8,128)(2,1)S(1)} %bitcast.8, ...), custom_call_target="tpu_custom_call" | custom-call | tf_op jit(solution)/shard_map/pallas_call | solution.py:518
  51.2 15.1 %shard_map.123 = bf16[64,160]{1,0:T(8,128)(2,1)S(1)} custom-call(bf16[8,80,128]{2,1,0:T(8,128)(2,1)S(1)} %get-tuple-element.24.parts), custom_call_target="tpu_custom_call" | custom-call | tf_op jit(solution)/shard_map/pallas_call | solution.py:530
  66.3 0.6 copy.14
Async XLA Ops:
  0.6 2.7 %copy-start = (bf16[1280,64]{0,1:T(8,128)(2,1)S(1)}, bf16[1280,64]{0,1:T(8,128)(2,1)}, u32[]{:S(2)}) copy-start(bf16[1280,64]{0,1:T(8,128)(2,1)} %param.10) | copy-start | bytes 491524

commit v3 on v2

--- a/solution.py
+++ b/solution.py
@@ -60,52 +60,27 @@
     return parts[0] if len(parts) == 1 else jnp.concatenate(parts, axis=0)
 
 
-def pick_kernel(ids, counts, down_hbm, picked, places, down, load_sem):
-    load = pltpu.make_async_copy(down_hbm, down, load_sem)
-    load.start()
-    low = lax.axis_index("blk") * OWN
-
-    first = jnp.int32(0)
-    for t in range(TILES):
-        live = counts[t]
-        packed = jnp.int32(0)
-        shift = jnp.int32(0)
-        for k in range(KMAX):
-            block = ids[t, k] - low
-            owned = (block >= 0) & (block < OWN) & (live > k)
-            packed = packed + jnp.where(owned, lax.shift_left(block + 1, shift), 0)
-            shift = shift + jnp.where(owned, 5, 0)
-        number = jnp.int32(0)
-        for j in range(PER):
-            place = lax.shift_right_logical(packed, jnp.int32(5 * j)) & 31
-            places[t * PER + j] = place
-            places[PAIRS + t * PER + j] = jnp.minimum(first + j, PAIRS - 1)
-            number = number + jnp.where(place > 0, 1, 0)
-        first = first + number
-
-    load.wait()
-    for t in range(TILES):
-        for j in range(PER):
-            block = jnp.maximum(places[t * PER + j] - 1, 0)
-            columns = pl.ds(pl.multiple_of(block * BLOCK, BLOCK), BLOCK)
-            picked[t, :, j * BLOCK : (j + 1) * BLOCK] = down[:, columns]
-
-
 def sum_kernel(
     side,
-    go,
-    picked,
+    ids,
+    counts,
+    go_hbm,
+    down_hbm,
     inp_hbm,
     up_hbm,
     gate_hbm,
     sg_hbm,
     su_hbm,
+    places,
     gh,
+    go,
     inp,
     up,
     gate,
     sg,
     su,
+    down,
+    picked,
     own,
     half_send,
     half_recv,
@@ -162,11 +137,50 @@
     loads = [
         pltpu.make_async_copy(source, target, load_sem.at[i])
         for i, (source, target) in enumerate(
-            ((inp_hbm, inp), (up_hbm, up), (gate_hbm, gate), (sg_hbm, sg), (su_hbm, su))
+            (
+                (down_hbm, down),
+                (go_hbm, go),
+                (inp_hbm, inp),
+                (up_hbm, up),
+                (gate_hbm, gate),
+                (sg_hbm, sg),
+                (su_hbm, su),
+            )
         )
     ]
     for load in loads:
         load.start()
+
+    low = me_z * OWN
+
+    first = jnp.int32(0)
+    for t in range(TILES):
+        live = counts[t]
+        packed = jnp.int32(0)
+        shift = jnp.int32(0)
+        for k in range(KMAX):
+            block = ids[t, k] - low
+            owned = (block >= 0) & (block < OWN) & (live > k)
+            packed = packed + jnp.where(owned, lax.shift_left(block + 1, shift), 0)
+            shift = shift + jnp.where(owned, 5, 0)
+        number = jnp.int32(0)
+        for j in range(PER):
+            place = lax.shift_right_logical(packed, jnp.int32(5 * j)) & 31
+            places[t * PER + j] = place
+            places[PAIRS + t * PER + j] = jnp.minimum(first + j, PAIRS - 1)
+            number = number + jnp.where(place > 0, 1, 0)
+        first = first + number
+
+    loads[0].wait()
+    for t in range(TILES):
+        wanted = [places[t * PER + j] for j in range(PER)]
+        found = [down[:, 0:BLOCK]] * PER
+        for b in range(1, OWN):
+            block = down[:, b * BLOCK : (b + 1) * BLOCK]
+            found = [jnp.where(w == b + 1, block, f) for w, f in zip(wanted, found)]
+        for j in range(PER):
+            picked[t, :, j * BLOCK : (j + 1) * BLOCK] = found[j]
+    loads[1].wait()
 
     def hidden_terms(t):
         tokens = go[:, pl.ds(pl.multiple_of(t * TILE, TILE), TILE)]
@@ -310,7 +324,7 @@
         for d in range(side):
             f_copy(d, 1 - core, n).wait_recv()
 
-    for load in loads:
+    for load in loads[2:]:
         load.wait()
     for i in range(HALF_TILES):
         h_copy(i).wait_send()
@@ -476,29 +490,24 @@
     anywhere = pl.BlockSpec(memory_space=pl.ANY)
     smem = pl.BlockSpec(memory_space=pltpu.SMEM)
     vmem = pl.BlockSpec(memory_space=pltpu.VMEM)
-    go = grad_out.T
     shape = jax.ShapeDtypeStruct
-    picked, places = pl.pallas_call(
-        pick_kernel,
-        out_shape=[shape((TILES, WIDTH, PER * BLOCK), BF16), shape((2 * PAIRS,), jnp.int32)],
-        in_specs=[smem, smem, anywhere],
-        out_specs=[vmem, smem],
-        scratch_shapes=[pltpu.VMEM((WIDTH, units), BF16), dma],
-        compiler_params=pltpu.CompilerParams(vmem_limit_bytes=VMEM_LIMIT),
-    )(*in_hbm(block_ids, counts, down_weight.T))
-    gh, inp, up, gate, sg, su = pl.pallas_call(
+    places, gh, go, inp, up, gate, sg, su = pl.pallas_call(
         functools.partial(sum_kernel, side),
         out_shape=[
+            shape((2 * PAIRS,), jnp.int32),
             shape((2, side * stride, BLOCK), BF16),
+            shape((WIDTH, tokens), BF16),
             shape((WIDTH, tokens), BF16),
             shape((WIDTH, units), BF16),
             shape((WIDTH, units), BF16),
             shape((PAIRS, TILE, BLOCK), BF16),
             shape((PAIRS, TILE, BLOCK), BF16),
         ],
-        in_specs=[vmem] * 2 + [anywhere] * 5,
-        out_specs=[vmem] * 6,
+        in_specs=[smem] * 2 + [anywhere] * 7,
+        out_specs=[smem] + [vmem] * 7,
         scratch_shapes=[
+            pltpu.VMEM((WIDTH, units), BF16),
+            pltpu.VMEM((TILES, WIDTH, PER * BLOCK), BF16),
             pltpu.VMEM((HALF, BLOCK), F32),
             pltpu.VMEM((HALF, BLOCK), BF16),
             pltpu.VMEM((HALF, BLOCK), BF16),
@@ -506,7 +515,7 @@
             pltpu.VMEM((side, chunk, BLOCK), BF16),
             pltpu.VMEM((stride, BLOCK), BF16),
             pltpu.VMEM((SUBS, side, piece, BLOCK), BF16),
-            dma((5,)),
+            dma((7,)),
             dma((HALF_TILES,)),
             dma((HALF_TILES,)),
         ]
@@ -514,7 +523,19 @@
         compiler_params=pltpu.CompilerParams(
             collective_id=0, has_side_effects=True, vmem_limit_bytes=VMEM_LIMIT
         ),
-    )(go, picked, *in_hbm(inputs.T, up_weight, gate_weight, saved_gate[0], saved_up[0]))
+    )(
+        *in_hbm(
+            block_ids,
+            counts,
+            grad_out.T,
+            down_weight.T,
+            inputs.T,
+            up_weight,
+            gate_weight,
+            saved_gate[0],
+            saved_up[0],
+        )
+    )
     grad_up, grad_gate, grad_down, parts = pl.pallas_call(
         functools.partial(grads_kernel, side, depth),
         out_shape=[shape((WIDTH, units), BF16)] * 3

time: 67.2 us -> 65.9 us (0.981)
  Pallas kernels: 65.7 us -> 64.4 us
    pallas_call x2 -> x1, Pallas kernels: 47.5 us -> 46.3 us  [shards(): pl.pallas_call(functools.partial(sum_kernel, side), out_shape=[shape((2 *...]
where the time goes in v3:
time: 65.9 us; the launch traced here: 65.7 us
  Pallas kernels  64.4 us (98%)
    pallas_call x1, Pallas kernels, shards(): pl.pallas_call(functools.partial(sum_kernel, side), out_shape=[shape((2 *...  46.3 us
    pallas_call x1, Pallas kernels, shards(): pl.pallas_call(functools.partial(parts_kernel, depth), out_shape=shape((W...  15 us
    pallas_call x1, Pallas kernels, shards(): pl.pallas_call(functools.partial(grads_kernel, side, depth), out_shape=[s...  3.11 us

profile of v3, /device:TPU:1, one launch (start us, length us, event | category | flops | bytes accessed | tf_op | source)
XLA Modules:
  0.0 65.7 jit_solution(11792956745146832184)
XLA Ops:
  0.6 46.3 %shard_map.120 = (s32[60]{0:T(128)S(1)}, bf16[2,2048,128]{2,1,0:T(8,128)(2,1)S(1)}, bf16[64,1280]{1,0:T(8,128)(2,1)S(1)}, bf16[64,1280]{1,0:T(8,128)(2,1)S(1)}, ...) custom-call(s32[10,24]{1,0:T(8,128)} %ids.1, ...), custom_call_target="tpu_custom_call" | custom-call | tf_op jit(solution)/shard_map/pallas_call | solution.py:494
  46.9 3.1 %shard_map.121 = (bf16[64,3584]{1,0:T(8,128)(2,1)}, bf16[64,3584]{1,0:T(8,128)(2,1)}, bf16[64,3584]{1,0:T(8,128)(2,1)}, bf16[8,80,128]{2,1,0:T(8,128)(2,1)S(1)}) custom-call(s32[60]{0:T(128)S(1)} %get-tuple-element.16.places, bf16[2,2048,128]{2,1,0:T(8,128)(2,1)S(1)} %get-tuple-element.17.gh, bf16[64,1280]{1,0:T(8,128)(2,1)S(1)} %get-tuple-element.18.go, ...), custom_call_target="tpu_custom_call" | custom-call | tf_op jit(solution)/shard_map/pallas_call | solution.py:539
  50.0 15.0 %shard_map.122 = bf16[64,160]{1,0:T(8,128)(2,1)S(1)} custom-call(bf16[8,80,128]{2,1,0:T(8,128)(2,1)S(1)} %get-tuple-element.24.parts), custom_call_target="tpu_custom_call" | custom-call | tf_op jit(solution)/shard_map/pallas_call | solution.py:551
  65.1 0.6 copy.14

commit v4 on v3

--- a/solution.py
+++ b/solution.py
@@ -62,6 +62,7 @@
 
 def sum_kernel(
     side,
+    depth,
     ids,
     counts,
     go_hbm,
@@ -72,13 +73,19 @@
     sg_hbm,
     su_hbm,
     places,
-    gh,
+    gx_out,
+    pairs,
     go,
     inp,
     up,
     gate,
     sg,
     su,
+    gh,
+    weights,
+    gx,
+    z_send,
+    z_recv,
     down,
     picked,
     own,
@@ -101,6 +108,8 @@
     d_rsem,
     f_ssem,
     f_rsem,
+    z_ssem,
+    z_rsem,
 ):
     chunk, subs = sizes(side)
     stride = stride_of(side)
@@ -132,6 +141,11 @@
         )
         pl.semaphore_signal(
             barrier, inc=1, device_id=(along_b(other(me_b, d)), me_z), device_id_type=MESH
+        )
+
+    for d in range(1, depth):
+        pl.semaphore_signal(
+            barrier, inc=1, device_id=(dp, (me_z + d) % depth), device_id_type=MESH
         )
 
     loads = [
@@ -210,7 +224,7 @@
             start = (i * PER + j) * TILE
             own[start : start + TILE, :] = mine[:, j * BLOCK : (j + 1) * BLOCK]
         if i == EARLY:
-            pl.semaphore_wait(barrier, 1 + 2 * (side - 1))
+            pl.semaphore_wait(barrier, 1 + 2 * (side - 1) + depth - 1)
             for k in range(HALF_TILES):
                 h_copy(k).start()
     for i in range(HALF_TILES):
@@ -283,6 +297,27 @@
     for n in steps:
         for d in order:
             a_copy(other(me_a, d), me_a, n).start()
+
+    loads[5].wait()
+    loads[6].wait()
+    for number in range(PAIRS):
+        t, j = divmod(number, PER)
+        slot = places[PAIRS + number]
+        live = jnp.where(places[number] > 0, jnp.float32(1), jnp.float32(0))
+        gate_value = sg[j]
+        up_value = su[j]
+        for c in range(j + 1, min(t * PER + j, PAIRS - 1) + 1):
+            gate_value = jnp.where(slot == c, sg[c], gate_value)
+            up_value = jnp.where(slot == c, su[c], up_value)
+        gate_value = gate_value.astype(F32)
+        up_value = up_value.astype(F32)
+        positive = jnp.maximum(gate_value, 0.0) * live
+        pairs[number, :, 0:BLOCK] = positive.astype(BF16)
+        pairs[number, :, BLOCK : 2 * BLOCK] = (
+            jnp.where(gate_value > 0, up_value, 0.0) * live
+        ).astype(BF16)
+        pairs[number, :, 2 * BLOCK : 3 * BLOCK] = (positive * up_value).astype(BF16)
+
     for n in steps:
         offset, number, piece = subs[n]
         rows = pl.ds(pl.multiple_of(me_a * chunk + offset, 16), number)
@@ -315,6 +350,19 @@
         for d in order:
             d_copy(other(me_a, d), me_a, n).start()
         f_copy(me_a, core, n).start()
+
+    loads[3].wait()
+    loads[4].wait()
+    for t in range(TILES):
+        wanted = [places[t * PER + j] for j in range(PER)]
+        for k, source in enumerate((up, gate)):
+            found = [source[:, 0:BLOCK]] * PER
+            for b in range(1, OWN):
+                block = source[:, b * BLOCK : (b + 1) * BLOCK]
+                found = [jnp.where(w == b + 1, block, f) for w, f in zip(wanted, found)]
+            for j in range(PER):
+                weights[t, :, (2 * j + k) * BLOCK : (2 * j + k + 1) * BLOCK] = found[j]
+
     for n in steps:
         for d in reversed(order):
             source = other(me_a, d)
@@ -324,79 +372,23 @@
         for d in range(side):
             f_copy(d, 1 - core, n).wait_recv()
 
-    for load in loads[2:]:
-        load.wait()
-    for i in range(HALF_TILES):
-        h_copy(i).wait_send()
-    for n in steps:
-        for d in range(1, side):
-            a_copy(other(me_a, d), me_a, n).wait_send()
-            b_copy(other(me_b, d), me_b, n).wait_send()
-            c_copy(other(me_b, d), me_b, n).wait_send()
-            d_copy(other(me_a, d), me_a, n).wait_send()
-        for d in range(side):
-            f_copy(d, core, n).wait_send()
-
-
-def grads_kernel(
-    side,
-    depth,
-    places,
-    gh,
-    go,
-    inp,
-    up,
-    gate,
-    sg,
-    su,
-    up_out,
-    gate_out,
-    down_out,
-    parts,
-    totals,
-    gx,
-):
-    chunk, _ = sizes(side)
-    stride = stride_of(side)
-    totals[...] = jnp.zeros_like(totals)
     for t in range(TILES):
         half, i = divmod(t, HALF_TILES)
-        weights = []
         values = []
-        tokens = slice(t * TILE, (t + 1) * TILE)
         for j in range(PER):
             number = t * PER + j
-            place = places[number]
-            slot = places[PAIRS + number]
-            live = jnp.where(place > 0, jnp.float32(1), jnp.float32(0))
-            block = jnp.maximum(place - 1, 0)
-            gate_value = sg[slot].astype(F32)
-            up_value = su[slot].astype(F32)
-            positive = jnp.maximum(gate_value, 0.0) * live
             value = rows_of(gh, half, i * PER + j, chunk, stride).astype(F32)
-            hidden = (positive * up_value).astype(BF16)
-            grad_up = (value * positive).astype(BF16)
-            grad_gate = (value * (jnp.where(gate_value > 0, up_value, 0.0) * live)).astype(BF16)
-            columns = pl.ds(pl.multiple_of(block * BLOCK, BLOCK), BLOCK)
-            weights += [up[:, columns], gate[:, columns]]
-            values += [grad_up, grad_gate]
-            pair = jnp.dot(
-                inp[:, tokens],
-                jnp.concatenate([grad_up, grad_gate], axis=1),
-                preferred_element_type=F32,
-            )
-            totals[0, block] += pair[:, 0:BLOCK]
-            totals[1, block] += pair[:, BLOCK : 2 * BLOCK]
-            totals[2, block] += jnp.dot(go[:, tokens], hidden, preferred_element_type=F32)
+            for k in range(2):
+                lanes = slice(k * BLOCK, (k + 1) * BLOCK)
+                grad = (value * pairs[number, :, lanes].astype(F32)).astype(BF16)
+                pairs[number, :, lanes] = grad
+                values.append(grad)
         gx[t] = lax.dot_general(
-            jnp.concatenate(weights, axis=1),
+            weights[t],
             jnp.concatenate(values, axis=1),
             (((1,), (1,)), ((), ())),
             preferred_element_type=F32,
         )
-    for i, out in enumerate((up_out, gate_out, down_out)):
-        for b in range(OWN):
-            out[:, b * BLOCK : (b + 1) * BLOCK] = totals[i, b].astype(BF16)
 
     lanes = lax.broadcasted_iota(jnp.int32, (WIDTH, TILE), 1)
     short = lax.broadcasted_iota(jnp.int32, (16, TILE), 1)
@@ -411,7 +403,7 @@
             )
         else:
             first = gx[q]
-        parts[to, 0:WIDTH, :] = first.astype(BF16)
+        z_send[to, 0:WIDTH, :] = first.astype(BF16)
         rest = jnp.zeros((16, TILE), F32)
         for s in range(4):
             shift = (32 * s - o) % TILE
@@ -419,49 +411,64 @@
             if shift:
                 moved = pltpu.roll(moved, shift, 1)
             rest = jnp.where(short // 32 == s, moved, rest)
-        parts[to, WIDTH:PART_ROWS, :] = rest.astype(BF16)
-
-
-def parts_kernel(depth, parts, gx_out, own, recv, load_sem, ssem, rsem):
-    dp = lax.axis_index("dp")
-    me_z = lax.axis_index("blk")
-    load = pltpu.make_async_copy(parts.at[me_z], own, load_sem)
-    load.start()
-
-    def other(d):
-        return (me_z + d) % depth
-
-    barrier = pltpu.get_barrier_semaphore()
-    for d in range(1, depth):
-        pl.semaphore_signal(barrier, inc=1, device_id=(dp, other(d)), device_id_type=MESH)
-    pl.semaphore_wait(barrier, depth - 1)
+        z_send[to, WIDTH:PART_ROWS, :] = rest.astype(BF16)
 
     def z_copy(to, slot):
         return pltpu.make_async_remote_copy(
-            src_ref=parts.at[to],
-            dst_ref=recv.at[slot],
-            send_sem=ssem.at[to],
-            recv_sem=rsem.at[slot],
+            src_ref=z_send.at[to],
+            dst_ref=z_recv.at[slot],
+            send_sem=z_ssem.at[to],
+            recv_sem=z_rsem.at[slot],
             device_id=(dp, to),
             device_id_type=MESH,
         )
 
-    order = sorted(range(1, depth), key=lambda d: -min(d, depth - d))
-    for d in order:
-        z_copy(other(d), me_z).start()
-    load.wait()
-    total = own[...].astype(F32)
-    for d in reversed(order):
-        source = other(d)
+    z_order = sorted(range(1, depth), key=lambda d: -min(d, depth - d))
+    for d in z_order:
+        z_copy((me_z + d) % depth, me_z).start()
+    total = z_send[me_z].astype(F32)
+    for d in reversed(z_order):
+        source = (me_z + d) % depth
         z_copy(source, source).wait_recv()
-        total = total + recv[source].astype(F32)
+        total = total + z_recv[source].astype(F32)
     gx_out[:, 0:TILE] = total[0:WIDTH, :].astype(BF16)
     rest = total[WIDTH:PART_ROWS, :]
     for s in range(4):
         moved = pltpu.roll(rest, TILE - 32 * s, 1) if s else rest
         gx_out[16 * s : 16 * (s + 1), TILE : TILE + 32] = moved[:, 0:32].astype(BF16)
     for d in range(1, depth):
-        z_copy(other(d), me_z).wait_send()
+        z_copy((me_z + d) % depth, me_z).wait_send()
+
+    loads[2].wait()
+    for i in range(HALF_TILES):
+        h_copy(i).wait_send()
+    for n in steps:
+        for d in range(1, side):
+            a_copy(other(me_a, d), me_a, n).wait_send()
+            b_copy(other(me_b, d), me_b, n).wait_send()
+            c_copy(other(me_b, d), me_b, n).wait_send()
+            d_copy(other(me_a, d), me_a, n).wait_send()
+        for d in range(side):
+            f_copy(d, core, n).wait_send()
+
+
+def grads_kernel(places, pairs, go, inp, up_out, gate_out, down_out, totals):
+    totals[...] = jnp.zeros_like(totals)
+    for number in range(PAIRS):
+        t = number // PER
+        tokens = slice(t * TILE, (t + 1) * TILE)
+        block = jnp.maximum(places[number] - 1, 0)
+        pair = jnp.dot(
+            inp[:, tokens], pairs[number, :, 0 : 2 * BLOCK], preferred_element_type=F32
+        )
+        totals[0, block] += pair[:, 0:BLOCK]
+        totals[1, block] += pair[:, BLOCK : 2 * BLOCK]
+        totals[2, block] += jnp.dot(
+            go[:, tokens], pairs[number, :, 2 * BLOCK : 3 * BLOCK], preferred_element_type=F32
+        )
+    for i, out in enumerate((up_out, gate_out, down_out)):
+        for b in range(OWN):
+            out[:, b * BLOCK : (b + 1) * BLOCK] = totals[i, b].astype(BF16)
 
 
 def in_hbm(*arrays):
@@ -491,21 +498,27 @@
     smem = pl.BlockSpec(memory_space=pltpu.SMEM)
     vmem = pl.BlockSpec(memory_space=pltpu.VMEM)
     shape = jax.ShapeDtypeStruct
-    places, gh, go, inp, up, gate, sg, su = pl.pallas_call(
-        functools.partial(sum_kernel, side),
+    places, grad_x, pairs, go, inp = pl.pallas_call(
+        functools.partial(sum_kernel, side, depth),
         out_shape=[
             shape((2 * PAIRS,), jnp.int32),
-            shape((2, side * stride, BLOCK), BF16),
+            shape((WIDTH, tokens // depth), BF16),
+            shape((PAIRS, TILE, 3 * BLOCK), BF16),
             shape((WIDTH, tokens), BF16),
             shape((WIDTH, tokens), BF16),
-            shape((WIDTH, units), BF16),
-            shape((WIDTH, units), BF16),
-            shape((PAIRS, TILE, BLOCK), BF16),
-            shape((PAIRS, TILE, BLOCK), BF16),
         ],
         in_specs=[smem] * 2 + [anywhere] * 7,
-        out_specs=[smem] + [vmem] * 7,
+        out_specs=[smem] + [vmem] * 4,
         scratch_shapes=[
+            pltpu.VMEM((WIDTH, units), BF16),
+            pltpu.VMEM((WIDTH, units), BF16),
+            pltpu.VMEM((PAIRS, TILE, BLOCK), BF16),
+            pltpu.VMEM((PAIRS, TILE, BLOCK), BF16),
+            pltpu.VMEM((2, side * stride, BLOCK), BF16),
+            pltpu.VMEM((TILES, WIDTH, 2 * PER * BLOCK), BF16),
+            pltpu.VMEM((TILES, WIDTH, TILE), F32),
+            pltpu.VMEM((depth, PART_ROWS, TILE), BF16),
+            pltpu.VMEM((depth, PART_ROWS, TILE), BF16),
             pltpu.VMEM((WIDTH, units), BF16),
             pltpu.VMEM((TILES, WIDTH, PER * BLOCK), BF16),
             pltpu.VMEM((HALF, BLOCK), F32),
@@ -519,7 +532,8 @@
             dma((HALF_TILES,)),
             dma((HALF_TILES,)),
         ]
-        + [dma((SUBS, side))] * 10,
+        + [dma((SUBS, side))] * 10
+        + [dma((depth,))] * 2,
         compiler_params=pltpu.CompilerParams(
             collective_id=0, has_side_effects=True, vmem_limit_bytes=VMEM_LIMIT
         ),
@@ -536,34 +550,14 @@
             saved_up[0],
         )
     )
-    grad_up, grad_gate, grad_down, parts = pl.pallas_call(
-        functools.partial(grads_kernel, side, depth),
-        out_shape=[shape((WIDTH, units), BF16)] * 3
-        + [shape((depth, PART_ROWS, TILE), BF16)],
-        in_specs=[smem] + [vmem] * 7,
-        out_specs=[vmem] * 4,
-        scratch_shapes=[
-            pltpu.VMEM((3, OWN, WIDTH, BLOCK), F32),
-            pltpu.VMEM((TILES, WIDTH, TILE), F32),
-        ],
+    grad_up, grad_gate, grad_down = pl.pallas_call(
+        grads_kernel,
+        out_shape=[shape((WIDTH, units), BF16)] * 3,
+        in_specs=[smem] + [vmem] * 3,
+        out_specs=[vmem] * 3,
+        scratch_shapes=[pltpu.VMEM((3, OWN, WIDTH, BLOCK), F32)],
         compiler_params=pltpu.CompilerParams(vmem_limit_bytes=VMEM_LIMIT),
-    )(places, gh, go, inp, up, gate, sg, su)
-    grad_x = pl.pallas_call(
-        functools.partial(parts_kernel, depth),
-        out_shape=shape((WIDTH, tokens // depth), BF16),
-        in_specs=[anywhere],
-        out_specs=vmem,
-        scratch_shapes=[
-            pltpu.VMEM((PART_ROWS, TILE), BF16),
-            pltpu.VMEM((depth, PART_ROWS, TILE), BF16),
-            dma,
-            dma((depth,)),
-            dma((depth,)),
-        ],
-        compiler_params=pltpu.CompilerParams(
-            collective_id=1, has_side_effects=True, vmem_limit_bytes=VMEM_LIMIT
-        ),
-    )(parts)
+    )(places, pairs, go, inp)
     return (grad_x.T, grad_up, grad_gate, grad_down.T)
 
 

time: 65.9 us -> 62.5 us (0.948)
  Pallas kernels: 64.4 us -> 61 us
    pallas_call x3 -> x2, Pallas kernels: 64.4 us -> 61 us  [the longest x1 58.5 us: shards(): pl.pallas_call(functools.partial(sum_kernel, side, depth), out_shape=[sha...]
where the time goes in v4:
time: 62.5 us; the launch traced here: 62.3 us
  Pallas kernels  61 us (98%)
  between operations  0.64 us (1%)
    pallas_call x1, Pallas kernels, shards(): pl.pallas_call(functools.partial(sum_kernel, side, depth), out_shape=[sha...  58.5 us
    pallas_call x1, Pallas kernels, shards(): pl.pallas_call(grads_kernel, out_shape=[shape((WIDTH, units), BF16)] * 3,...  2.52 us

profile of v4, /device:TPU:1, one launch (start us, length us, event | category | flops | bytes accessed | tf_op | source)
XLA Modules:
  0.0 62.3 jit_solution(3800194558386502007)
XLA Ops:
  0.6 58.5 %shard_map.120 = (s32[60]{0:T(128)S(1)}, bf16[64,160]{1,0:T(8,128)(2,1)S(1)}, bf16[30,128,384]{2,1,0:T(8,128)(2,1)S(1)}, bf16[64,1280]{1,0:T(8,128)(2,1)S(1)}, bf16[64,1280]{1,0:T(8,128)(2,1)S(1)}) custom-call(s32[10,24]{1,0:T(8,128)} %ids.1, s32[10]{0:T(128)} %counts.1, bf16[64,1280]{1,0:T(8,128)(2,1)} %bitcast.11, bf16[64,3584]{1,0:T(8,128)(2,1)} %bitcast.10, ...), custom_call_target="tpu_custom_call" | custom-call | tf_op jit(solution)/shard_map/pallas_call | solution.py:501
  59.1 2.5 %shard_map.121 = (bf16[64,3584]{1,0:T(8,128)(2,1)}, bf16[64,3584]{1,0:T(8,128)(2,1)}, bf16[64,3584]{1,0:T(8,128)(2,1)}) custom-call(s32[60]{0:T(128)S(1)} %get-tuple-element.13.places, bf16[30,128,384]{2,1,0:T(8,128)(2,1)S(1)} %get-tuple-element.14.pairs, bf16[64,1280]{1,0:T(8,128)(2,1)S(1)} %get-tuple-element.15.go, bf16[64,1280]{1,0:T(8,128)(2,1)S(1)} %get-tuple-element.16.inp), custom_call_target="tpu_custom_call" | custom-call | tf_op jit(solution)/shard_map/pallas_call | solution.py:553
  61.7 0.6 copy.14

commit v5 on v4

--- a/solution.py
+++ b/solution.py
@@ -368,12 +368,14 @@
             source = other(me_a, d)
             d_copy(source, source, n).wait_recv()
             f_copy(source, core, n).start()
-    for n in steps:
-        for d in range(side):
-            f_copy(d, 1 - core, n).wait_recv()
-
-    for t in range(TILES):
-        half, i = divmod(t, HALF_TILES)
+    for part in range(2 * HALF_TILES):
+        if part == HALF_TILES:
+            for n in steps:
+                for d in range(side):
+                    f_copy(d, 1 - core, n).wait_recv()
+        i = part % HALF_TILES
+        half = core if part < HALF_TILES else 1 - core
+        t = half * HALF_TILES + i
         values = []
         for j in range(PER):
             number = t * PER + j

time: 62.5 us -> 62.7 us (level)
  no operation moved by 1% of the time
where the time goes in v5:
time: 62.7 us; the launch traced here: 62.5 us
  Pallas kernels  61.3 us (98%)
  between operations  0.64 us (1%)
    pallas_call x1, Pallas kernels, shards(): pl.pallas_call(functools.partial(sum_kernel, side, depth), out_shape=[sha...  58.7 us
    pallas_call x1, Pallas kernels, shards(): pl.pallas_call(grads_kernel, out_shape=[shape((WIDTH, units), BF16)] * 3,...  2.53 us

profile of v5, /device:TPU:1, one launch (start us, length us, event | category | flops | bytes accessed | tf_op | source)
XLA Modules:
  0.0 62.5 jit_solution(6134345610791267153)
XLA Ops:
  0.6 58.7 %shard_map.120 = (s32[60]{0:T(128)S(1)}, bf16[64,160]{1,0:T(8,128)(2,1)S(1)}, bf16[30,128,384]{2,1,0:T(8,128)(2,1)S(1)}, bf16[64,1280]{1,0:T(8,128)(2,1)S(1)}, bf16[64,1280]{1,0:T(8,128)(2,1)S(1)}) custom-call(s32[10,24]{1,0:T(8,128)} %ids.1, s32[10]{0:T(128)} %counts.1, bf16[64,1280]{1,0:T(8,128)(2,1)} %bitcast.11, bf16[64,3584]{1,0:T(8,128)(2,1)} %bitcast.10, ...), custom_call_target="tpu_custom_call" | custom-call | tf_op jit(solution)/shard_map/pallas_call | solution.py:503
  59.4 2.5 %shard_map.121 = (bf16[64,3584]{1,0:T(8,128)(2,1)}, bf16[64,3584]{1,0:T(8,128)(2,1)}, bf16[64,3584]{1,0:T(8,128)(2,1)}) custom-call(s32[60]{0:T(128)S(1)} %get-tuple-element.13.places, bf16[30,128,384]{2,1,0:T(8,128)(2,1)S(1)} %get-tuple-element.14.pairs, bf16[64,1280]{1,0:T(8,128)(2,1)S(1)} %get-tuple-element.15.go, bf16[64,1280]{1,0:T(8,128)(2,1)S(1)} %get-tuple-element.16.inp), custom_call_target="tpu_custom_call" | custom-call | tf_op jit(solution)/shard_map/pallas_call | solution.py:555
  61.9 0.6 copy.14
